TPU v7x, 32 devices: a whole 2x2x4 slice. The times are simulated.
32 devices in a mesh: expert: 4 (over y, x), req: 8 (over z, core).
Axes of the slice: x: 2, y: 2, z: 4, core: 2. Of those that a mesh axis runs over, the one named last changes fastest.
Arguments:
- queries: bfloat16 [8192, 1024], P(('expert', 'req')), may hold values from -82 to 82
- self_kv: bfloat16 [8192, 2048], P(('expert', 'req')), may hold values from -4 to 4
- kv_pages: bfloat16 [32, 128, 2048], P(('expert', 'req')), may hold values from -4 to 4
- page_table: int32 [4, 8], P('expert'), may hold values from 0 to 7, as said below
- lengths: int32 [8192], P(('expert', 'req')), may hold values from 1 to 1024
- routes: int32 [8192, 2], P(('expert', 'req')), may hold values from 0 to 3, all different within a row
- residual: bfloat16 [8192, 1024], P(('expert', 'req')), may hold values from -20 to 20
- w_attn_out: bfloat16 [1024, 1024], replicated, may hold values from -0.1875 to 0.1875
- gain_attn: bfloat16 [1024], replicated, may hold values from 0.25 to 1.75
- w_router: bfloat16 [1024, 4], replicated, may hold values from -0.1875 to 0.1875
- w_in: bfloat16 [4, 1024, 2816], P('expert'), may hold values from -0.1875 to 0.1875
- w_out: bfloat16 [4, 1408, 1024], P('expert'), may hold values from -0.15625 to 0.15625
- gain_out: bfloat16 [1024], replicated, may hold values from 0.25 to 1.75
Outputs:
- layer_out: bfloat16 [8192, 1024], P(('expert', 'req'))
Inputs may be any that keep to these rules, and one draw needn't show every extreme that they name: Each row of page_table is a permutation of 0 to 7.
All inputs are finite; a program needn't handle non-finite values.
Results may differ from a plain program's by a relative error of at most 0.01.
Values may be sent and summed in bfloat16 or wider, within the bound.
A program may use at most 128 MiB of HBM per device.

v0:
```python
import math
import jax
import jax.numpy as jnp
from jax import lax
from jax.sharding import PartitionSpec as P

HEADS = 16
HEAD_DIM = 64
TOP = 2
PAGE = 128
HD = 1024
norm_eps = 1e-06


def block_size(total_count, largest):
    chosen = min(total_count, largest)
    while total_count % chosen:
        chosen -= 1
    return chosen


def key_positions(table_row, key_count, page_len):
    logical = jnp.arange(table_row.shape[0], dtype=jnp.int32)
    inverse = jnp.sum(
        jnp.where(table_row[:, None] == logical[None, :], logical[:, None], 0), axis=0
    )
    flat_index = jnp.arange(key_count, dtype=jnp.int32)
    page_index = flat_index // page_len
    logical_page = jnp.sum(
        jnp.where(page_index[:, None] == logical[None, :], inverse[None, :], 0), axis=1
    )
    return logical_page * page_len + flat_index % page_len


def rms_scale(values, gain_row):
    mean_square = jnp.mean(values * values, axis=-1, keepdims=True)
    return values * lax.rsqrt(mean_square + norm_eps) * gain_row.astype(jnp.float32)


def route_block(route_rows, cap_size, expert_count):
    onehot = (
        route_rows[:, :, None] == jnp.arange(expert_count, dtype=jnp.int32)[None, None, :]
    ).astype(jnp.int32)
    ordered = onehot.transpose(1, 0, 2).reshape(-1, expert_count)
    total = ordered.shape[0]
    before = jnp.arange(total)[:, None] > jnp.arange(total)[None, :]
    earlier = jnp.dot(
        before.astype(jnp.bfloat16),
        ordered.astype(jnp.bfloat16),
        preferred_element_type=jnp.float32,
    ).astype(jnp.int32)
    position = jnp.sum(earlier * ordered, axis=1).reshape(route_rows.shape[1], route_rows.shape[0])
    kept_mask = position < cap_size
    slot_ids = jnp.where(kept_mask, route_rows.T * cap_size + position, -1)
    return (onehot, kept_mask, slot_ids)


def on_device(
    queries,
    self_kv,
    kv_pages,
    page_table,
    lengths,
    routes,
    residual,
    w_attn_out,
    gain_attn,
    w_router,
    w_in,
    w_out,
    gain_out,
):
    row_count = queries.shape[0]
    scale_qk = 1.0 / math.sqrt(HEAD_DIM)
    table_row = page_table[0]
    page_rows = kv_pages.reshape(-1, kv_pages.shape[-1])
    query_h = queries.reshape(row_count, HEADS, HEAD_DIM)
    own_key = self_kv[:, :HD].reshape(row_count, HEADS, HEAD_DIM)
    own_value = self_kv[:, HD:].reshape(row_count, HEADS, HEAD_DIM)
    own_score = (
        jnp.einsum("rhd,rhd->hr", query_h, own_key, preferred_element_type=jnp.float32) * scale_qk
    )
    start_value = jnp.swapaxes(own_value, 0, 1).astype(jnp.float32)
    initial = (own_score, jnp.ones_like(own_score), start_value)
    page_piece = lax.all_gather(page_rows, "req", axis=0, tiled=True)
    piece_len = page_piece.shape[0]
    step_len = block_size(piece_len, 512)
    positions = key_positions(table_row, piece_len, PAGE)
    blocks = page_piece.reshape(piece_len // step_len, step_len, page_piece.shape[1])
    block_pos = positions.reshape(piece_len // step_len, step_len)

    def add_block(running, block_items):
        highest, weight_sum, weighted = running
        block_rows, block_place = block_items
        key_rows = block_rows[:, :HD].reshape(step_len, HEADS, HEAD_DIM)
        value_rows = block_rows[:, HD:].reshape(step_len, HEADS, HEAD_DIM)
        scores = (
            jnp.einsum("rhd,khd->hrk", query_h, key_rows, preferred_element_type=jnp.float32)
            * scale_qk
        )
        visible = block_place[None, :] < lengths[:, None]
        masked = jnp.where(visible[None], scores, -jnp.inf)
        new_high = jnp.maximum(highest, jnp.max(masked, axis=2))
        factor = jnp.exp(highest - new_high)
        weights = jnp.exp(masked - new_high[:, :, None])
        weight_sum = weight_sum * factor + jnp.sum(weights, axis=2)
        weighted = weighted * factor[:, :, None] + jnp.einsum(
            "hrk,khd->hrd",
            weights.astype(jnp.bfloat16),
            value_rows,
            preferred_element_type=jnp.float32,
        )
        return ((new_high, weight_sum, weighted), None)

    result, unused = lax.scan(add_block, initial, (blocks, block_pos))
    highest, weight_sum, weighted = result
    attended = (
        (weighted / weight_sum[:, :, None])
        .transpose(1, 0, 2)
        .reshape(row_count, HD)
        .astype(jnp.bfloat16)
    )
    residual_sum = residual.astype(jnp.float32) + jnp.dot(
        attended, w_attn_out, preferred_element_type=jnp.float32
    )
    normed = rms_scale(residual_sum, gain_attn).astype(jnp.bfloat16)
    logits = jnp.dot(normed, w_router, preferred_element_type=jnp.float32)
    experts_all = w_router.shape[1]
    cap_size = (5 * row_count * TOP + 4 * experts_all - 1) // (4 * experts_all)
    onehot, kept_mask, slot_ids = route_block(routes, cap_size, experts_all)
    picked = jnp.sum(jnp.where(onehot > 0, logits[:, None, :], 0.0), axis=2)
    gate_values = jax.nn.sigmoid(picked - picked[:, ::-1])
    slot_range = jnp.arange(experts_all * cap_size, dtype=jnp.int32)
    assign = jnp.sum(
        (slot_ids[:, None, :] == slot_range[None, :, None]).astype(jnp.bfloat16), axis=0
    )
    model_width = normed.shape[1]
    buffer = (
        jnp.dot(assign, normed, preferred_element_type=jnp.float32)
        .astype(jnp.bfloat16)
        .reshape(experts_all, cap_size, model_width)
    )
    arrived = lax.all_to_all(buffer, "expert", split_axis=0, concat_axis=0, tiled=True)
    slot_count = arrived.shape[1]
    local_experts = w_in.shape[0]
    hidden_width = w_out.shape[1]
    grouped = arrived.reshape(-1, local_experts, slot_count, model_width)
    inner_act = jnp.einsum("slnd,ldf->slnf", grouped, w_in, preferred_element_type=jnp.float32)
    hidden = (
        jax.nn.gelu(inner_act[..., :hidden_width], approximate=True) * inner_act[..., hidden_width:]
    ).astype(jnp.bfloat16)
    outcome = jnp.einsum(
        "slnf,lfd->slnd", hidden, w_out, preferred_element_type=jnp.float32
    ).astype(jnp.bfloat16)
    expert_done = outcome.reshape(-1, slot_count, model_width)
    collected = lax.all_to_all(expert_done, "expert", split_axis=0, concat_axis=0, tiled=True)
    flat_rows = collected.reshape(-1, model_width)
    picked_rows = flat_rows[jnp.maximum(slot_ids, 0)]
    gate_kept = jnp.where(kept_mask, gate_values.T, 0.0)
    mixture = jnp.sum(picked_rows.astype(jnp.float32) * gate_kept[:, :, None], axis=0)
    return rms_scale(residual_sum + mixture, gain_out).astype(jnp.bfloat16)


def solution(mesh):
    in_specs = (
        P(("expert", "req"), None),
        P(("expert", "req"), None),
        P(("expert", "req"), None, None),
        P("expert", None),
        P(("expert", "req")),
        P(("expert", "req"), None),
        P(("expert", "req"), None),
        P(),
        P(),
        P(),
        P("expert", None, None),
        P("expert", None, None),
        P(),
    )
    out_specs = P(("expert", "req"), None)
    return jax.shard_map(
        on_device, mesh=mesh, in_specs=in_specs, out_specs=out_specs, check_vma=False
    )
```

profile of v0, /device:TPU:0, one launch (start us, length us, event | category | flops | bytes accessed | tf_op | source)
XLA Modules:
  0.0 183.1 jit_solution(15243660066245395391)
XLA Ops:
  6.6 0.7 all-gather.3.cloned.1.call-update
  7.3 2.5 %slice_convert_fusion = (f32[256,1024]{1,0:T(8,128)}, bf16[256,1024]{1,0:T(8,128)(2,1)S(1)}) fusion(bf16[256,2048]{1,0:T(8,128)(2,1)} %param.16), kind=kLoop, calls=%fused_computation.55 | loop fusion | flops 262144 | bytes 2621440 | tf_op jit(solution)/shard_map/convert_element_type | solution.py:83
  9.7 1.0 copy.42
  10.7 1.2 copy.40
  12.0 2.6 %copy.29 = f32[256,1024]{0,1:T(8,128)} copy(f32[256,1024]{1,0:T(8,128)} %get-tuple-element.119) | data formatting | bytes 2097152 | tf_op jit(solution)/shard_map/convert_element_type | solution.py:83
  15.7 0.6 maximum_bitcast_fusion
  16.3 1.0 fusion.43
  17.3 1.2 fusion.42
  18.5 0.6 fusion.44
  19.1 0.6 broadcast_multiply_fusion
  19.7 39.1 %all-gather.3.cloned.1.call-done = bf16[1,1024,2048]{2,1,0:T(8,128)(2,1)} async-done(((bf16[1,128,2048]{2,1,0:T(8,128)(2,1)}), bf16[1,1024,2048]{2,1,0:T(8,128)(2,1)}) %all-gather.3.cloned.1.call-update) | async-done | bytes 4194320 | tf_op jit(solution)/shard_map/all_gather | solution.py:85
  58.9 54.3 %while.15 = (s32[]{:T(128)}, f32[16,256]{1,0:T(8,128)}, f32[16,256]{1,0:T(8,128)}, f32[16,256,64]{1,2,0:T(8,128)}, s32[2,512]{1,0:T(2,128)}, /*index=5*/s32[256]...) while((s32[]{:T(128)}, f32[16,256]{1,0:T(8,128)}, ...), condition=%wide.region_5.6_spmd.clone, body=%wide.region_2.5_spmd.clone.sunk | while | flops 560607232 | bytes 76881064 | solution.py:115
  58.9 0.7 constant_dynamic-slice_fusion.4
  59.5 0.8 broadcast_compare_fusion.3
  60.4 3.1 %constant_dynamic-slice_fusion.5 = bf16[1,512,2048]{2,1,0:T(8,128)(2,1)} fusion(bf16[2,512,2048]{2,1,0:T(8,128)(2,1)} %get-tuple-element.210, s32[]{:T(128)} %get-tuple-element.194), kind=kLoop, calls=%fused_computation.13.clone.1 | loop fusion | bytes 4194308 | tf_op jit(solution)/shard_map/while/body/jit(dynamic_index_in_dim)/dynamic_slice | solution.py:115
  63.5 3.9 %copy.46 = bf16[1,512,2048]{1,2,0:T(8,128)(2,1)} copy(bf16[1,512,2048]{2,1,0:T(8,128)(2,1)} %constant_dynamic-slice_fusion.5) | data formatting | bytes 4194304 | tf_op jit(solution)/shard_map/while/body/jit(dynamic_index_in_dim)/dynamic_slice | solution.py:115
  67.4 2.6 %fusion.80 = (bf16[512,1024]{0,1:T(8,128)(2,1)}, bf16[512,1024]{0,1:T(8,128)(2,1)S(1)}) fusion(bf16[512,2048]{0,1:T(8,128)(2,1)} %bitcast.102), kind=kLoop, calls=%fused_computation.94.clone.1 | loop fusion | bytes 4194304 | tf_op jit(solution)/shard_map/while/body/eval_jaxpr/slice | solution.py:96
  70.1 1.5 fusion.81
  71.6 3.2 %copy-done.1 = f32[16,512,256]{2,1,0:T(8,128)} copy-done((f32[16,512,256]{2,1,0:T(8,128)}, f32[16,512,256]{2,1,0:T(8,128)S(1)}, u32[]{:S(2)}) %copy-start.1) | copy-done | bytes 8388632 | tf_op jit(solution)/shard_map/while
  74.8 2.3 %fusion.82 = f32[16,256]{1,0:T(8,128)} fusion(f32[16,512,256]{2,1,0:T(8,128)S(1)} %get-tuple-element.180, f32[16,256]{1,0:T(8,128)S(1)} %max.10, pred[256,512]{0,1:T(8,128)(4,1)S(1)} %broadcast_compare_fusion.3), kind=kLoop, calls=%fused_computation.4.clone.1 | loop fusion | flops 8384512 | bytes 8552448 | tf_op jit(solution)/shard_map/while/body/eval_jaxpr/reduce_sum | solution.py:106
  77.1 1.3 fusion.83
  78.4 7.0 %fusion.84 = f32[16,256,64]{1,2,0:T(8,128)} fusion(bf16[512,16,64]{0,2,1:T(8,128)(2,1)} %bitcast.105, f32[16,512,256]{2,1,0:T(8,128)} %copy-done.1, f32[16,256]{1,0:T(8,128)S(1)} %max.10, pred[256,512]{0,1:T(8,128)(4,1)S(1)} %broadcast_compare_fusion.3, f32[16,256,64]{1,2,0:T(8,128)} %get-tuple-element.197, f32[16,256]{1,0:T(8,128)S(1)} %get-tuple-element.183), kind=kOutput, calls=%fused_computation.8.clone.1 | convolution fusion | flops 277348352 | bytes 11698176 | tf_op jit(solution)/shard_map/while/body/eval_jaxpr/hrk,khd->hrd/dot_general | solution.py:107
  85.4 0.6 copy.56
  86.0 0.7 constant_dynamic-slice_fusion.4
  86.7 0.8 broadcast_compare_fusion.3
  87.5 3.1 %constant_dynamic-slice_fusion.5 = bf16[1,512,2048]{2,1,0:T(8,128)(2,1)} fusion(bf16[2,512,2048]{2,1,0:T(8,128)(2,1)} %get-tuple-element.210, s32[]{:T(128)} %get-tuple-element.194), kind=kLoop, calls=%fused_computation.13.clone.1 | loop fusion | bytes 4194308 | tf_op jit(solution)/shard_map/while/body/jit(dynamic_index_in_dim)/dynamic_slice | solution.py:115
  90.7 3.9 %copy.46 = bf16[1,512,2048]{1,2,0:T(8,128)(2,1)} copy(bf16[1,512,2048]{2,1,0:T(8,128)(2,1)} %constant_dynamic-slice_fusion.5) | data formatting | bytes 4194304 | tf_op jit(solution)/shard_map/while/body/jit(dynamic_index_in_dim)/dynamic_slice | solution.py:115
  94.6 2.6 %fusion.80 = (bf16[512,1024]{0,1:T(8,128)(2,1)}, bf16[512,1024]{0,1:T(8,128)(2,1)S(1)}) fusion(bf16[512,2048]{0,1:T(8,128)(2,1)} %bitcast.102), kind=kLoop, calls=%fused_computation.94.clone.1 | loop fusion | bytes 4194304 | tf_op jit(solution)/shard_map/while/body/eval_jaxpr/slice | solution.py:96
  97.2 1.5 fusion.81
  98.8 3.2 %copy-done.1 = f32[16,512,256]{2,1,0:T(8,128)} copy-done((f32[16,512,256]{2,1,0:T(8,128)}, f32[16,512,256]{2,1,0:T(8,128)S(1)}, u32[]{:S(2)}) %copy-start.1) | copy-done | bytes 8388632 | tf_op jit(solution)/shard_map/while
  102.0 2.3 %fusion.82 = f32[16,256]{1,0:T(8,128)} fusion(f32[16,512,256]{2,1,0:T(8,128)S(1)} %get-tuple-element.180, f32[16,256]{1,0:T(8,128)S(1)} %max.10, pred[256,512]{0,1:T(8,128)(4,1)S(1)} %broadcast_compare_fusion.3), kind=kLoop, calls=%fused_computation.4.clone.1 | loop fusion | flops 8384512 | bytes 8552448 | tf_op jit(solution)/shard_map/while/body/eval_jaxpr/reduce_sum | solution.py:106
  104.2 1.4 fusion.83
  105.6 7.0 %fusion.84 = f32[16,256,64]{1,2,0:T(8,128)} fusion(bf16[512,16,64]{0,2,1:T(8,128)(2,1)} %bitcast.105, f32[16,512,256]{2,1,0:T(8,128)} %copy-done.1, f32[16,256]{1,0:T(8,128)S(1)} %max.10, pred[256,512]{0,1:T(8,128)(4,1)S(1)} %broadcast_compare_fusion.3, f32[16,256,64]{1,2,0:T(8,128)} %get-tuple-element.197, f32[16,256]{1,0:T(8,128)S(1)} %get-tuple-element.183), kind=kOutput, calls=%fused_computation.8.clone.1 | convolution fusion | flops 277348352 | bytes 11698176 | tf_op jit(solution)/shard_map/while/body/eval_jaxpr/hrk,khd->hrd/dot_general | solution.py:107
  112.6 0.6 copy.56
  113.2 1.5 divide_convert_fusion
  114.7 2.7 %multiply_reduce_fusion.1 = (f32[256]{0:T(256)S(1)}, f32[256,1024]{1,0:T(8,128)S(1)}) fusion(bf16[256,1024]{0,1:T(8,128)(2,1)S(1)} %bitcast.110, bf16[1024,1024]{1,0:T(8,128)(2,1)} %param.22, bf16[256,1024]{1,0:T(8,128)(2,1)} %param.21), kind=kOutput, calls=%fused_computation.51 | convolution fusion | flops 537919232 | bytes 4195328 | tf_op jit(solution)/shard_map/dot_general | solution.py:123
  117.4 1.0 copy-done.2
  118.4 0.6 convolution_convert_fusion
  119.0 20.6 %all_to_all.10 = bf16[4,160,1024]{2,1,0:T(8,128)(2,1)S(1)} all-to-all(bf16[4,160,1024]{2,1,0:T(8,128)(2,1)S(1)} %bitcast.107), channel_id=1, replica_groups=mesh['expert'=4,'req'=8] {'expert'}, dimensions={0} | all-to-all | bytes 2621440 | tf_op jit(solution)/shard_map/all_to_all | solution.py:143
  139.6 3.9 %fusion.14 = f32[4,1,160,2816]{3,2,0,1:T(8,128)S(1)} fusion(bf16[4,160,1024]{2,1,0:T(8,128)(2,1)S(1)} %all_to_all.10, bf16[1,1024,2816]{2,1,0:T(8,128)(2,1)S(1)} %bitcast.116), kind=kOutput, calls=%fused_computation.20 | convolution fusion | flops 3690987520 | bytes 14286848 | tf_op jit(solution)/shard_map/slnd,ldf->slnf/dot_general | solution.py:148
  143.5 3.6 %fusion.34 = bf16[4,160,1024]{2,1,0:T(8,128)(2,1)} fusion(bf16[1,1408,1024]{2,1,0:T(8,128)(2,1)S(1)} %copy-done, f32[4,1,160,2816]{3,2,0,1:T(8,128)S(1)} %fusion.14), kind=kOutput, calls=%fused_computation.39 | convolution fusion | flops 1855160320 | bytes 11403264 | tf_op jit(solution)/shard_map/slnf,lfd->slnd/dot_general | solution.py:152
  147.2 4.4 %all-to-all-start.1 = ((bf16[4,160,1024]{2,1,0:T(8,128)(2,1)}), bf16[4,160,1024]{2,1,0:T(8,128)(2,1)}, u32[]{:S(2)}, u32[]{:S(2)}) async-start(bf16[4,160,1024]{2,1,0:T(8,128)(2,1)} %fusion.34), calls=%async_computation.1 | async-start | bytes 2621440 | tf_op jit(solution)/shard_map/all_to_all | solution.py:156
  151.7 1.5 fusion.56
  153.4 13.9 %all-to-all-done.1 = bf16[4,160,1024]{2,1,0:T(8,128)(2,1)} async-done(((bf16[4,160,1024]{2,1,0:T(8,128)(2,1)}), bf16[4,160,1024]{2,1,0:T(8,128)(2,1)}, u32[]{:S(2)}, u32[]{:S(2)}) %all-to-all-start.1) | async-done | bytes 1310752 | tf_op jit(solution)/shard_map/all_to_all | solution.py:156
  167.3 5.0 %gather_fusion = bf16[512,1024]{1,0:T(8,128)(2,1)} fusion(bf16[640,1024]{1,0:T(8,128)(2,1)} %bitcast.25, s32[1024]{0:T(1024)S(1)} %pad_clamp_fusion), kind=kCustom, calls=%fused_computation | custom fusion | bytes 2099200 | tf_op jit(solution)/shard_map/gather | solution.py:158
  172.3 1.6 fusion.28
  173.8 1.4 multiply_reduce_fusion
  175.3 1.0 multiply_convert_fusion
  (57 shorter events, 1.3 us)
Async XLA Ops:
  6.5 137.0 %copy-start = (bf16[1,1408,1024]{2,1,0:T(8,128)(2,1)S(1)}, bf16[1,1408,1024]{2,1,0:T(8,128)(2,1)}, u32[]{:S(2)}) copy-start(bf16[1,1408,1024]{2,1,0:T(8,128)(2,1)} %param.26) | copy-start | bytes 8650756
  6.5 8.1 %copy-start.14 = (s32[1,8]{1,0:T(1,128)S(1)}, s32[1,8]{1,0:T(1,128)}, u32[]{:S(2)}) copy-start(s32[1,8]{1,0:T(1,128)} %param.18) | copy-start | bytes 100
  6.5 8.3 %copy-start.12 = (bf16[1024]{0:T(1024)(128)(2,1)S(1)}, bf16[1024]{0:T(1024)(128)(2,1)}, u32[]{:S(2)}) copy-start(bf16[1024]{0:T(1024)(128)(2,1)} %param.23) | copy-start | bytes 6148
  6.5 8.8 %copy-start.6 = (s32[256,2]{0,1:T(2,128)S(1)}, s32[256,2]{0,1:T(2,128)}, u32[]{:S(2)}) copy-start(s32[256,2]{0,1:T(2,128)} %param.20) | copy-start | bytes 6148
  6.5 52.3 %all-gather.3.cloned.1.call-start = ((), (), s32[]{:S(2)}) async-start(), calls=%async_computation.2 | async-start | bytes 4718592 | tf_op jit(solution)/shard_map/all_gather | solution.py:85
  15.7 43.2 %copy-start.8 = (s32[2,256]{1,0:T(2,128)}, s32[2,256]{1,0:T(2,128)S(1)}, u32[]{:S(2)}) copy-start(s32[2,256]{1,0:T(2,128)S(1)} %reshape.127) | copy-start | bytes 6148
  70.1 1.5 copy-start.3
  71.6 3.2 %copy-start.1 = (f32[16,512,256]{2,1,0:T(8,128)}, f32[16,512,256]{2,1,0:T(8,128)S(1)}, u32[]{:S(2)}) copy-start(f32[16,512,256]{2,1,0:T(8,128)S(1)} %get-tuple-element.180) | copy-start | bytes 25165828 | tf_op jit(solution)/shard_map/while
  97.2 1.5 copy-start.3
  98.7 3.2 %copy-start.1 = (f32[16,512,256]{2,1,0:T(8,128)}, f32[16,512,256]{2,1,0:T(8,128)S(1)}, u32[]{:S(2)}) copy-start(f32[16,512,256]{2,1,0:T(8,128)S(1)} %get-tuple-element.180) | copy-start | bytes 25165828 | tf_op jit(solution)/shard_map/while
  113.2 5.2 %copy-start.4 = (bf16[640,256]{1,0:T(8,128)(2,1)S(1)}, bf16[640,256]{1,0:T(8,128)(2,1)}, u32[]{:S(2)}) copy-start(bf16[640,256]{1,0:T(8,128)(2,1)} %fusion.43) | copy-start | bytes 983044
  113.2 5.2 %copy-start.5 = (f32[1024]{0:T(1024)S(1)}, f32[1024]{0:T(1024)}, u32[]{:S(2)}) copy-start(f32[1024]{0:T(1024)} %convert_element_type.81) | copy-start | bytes 12292
  113.2 26.4 %slice-start = ((s8[5767168]{0:T(1024)(128)(4,1)}), s8[4194304]{0:T(1024)(128)(4,1)S(1)}, s32[]{:S(2)}) async-start(s8[5767168]{0:T(1024)(128)(4,1)} %bitcast.115), calls=%async_computation.3 | async-start | bytes 8388608
  114.7 24.9 %slice-start.1 = ((s8[5767168]{0:T(1024)(128)(4,1)}), s8[1572864]{0:T(1024)(128)(4,1)S(1)}, s32[]{:S(2)}) async-start(s8[5767168]{0:T(1024)(128)(4,1)} %bitcast.115), calls=%async_computation.4 | async-start | bytes 3145728
  117.4 1.0 copy-start.2
  143.5 8.1 %copy-start.11 = (s32[1,2,2,128]{3,2,1,0:T(2,128)S(1)}, s32[1,2,2,128]{3,2,1,0:T(2,128)}, u32[]{:S(2)}) copy-start(s32[1,2,2,128]{3,2,1,0:T(2,128)} %get-tuple-element.113) | copy-start | bytes 6148
  143.5 8.1 %copy-start.13 = (bf16[1024]{0:T(1024)(128)(2,1)S(1)}, bf16[1024]{0:T(1024)(128)(2,1)}, u32[]{:S(2)}) copy-start(bf16[1024]{0:T(1024)(128)(2,1)} %param.27) | copy-start | bytes 6148
  143.5 8.1 %copy-start.10 = (bf16[1024,4]{0,1:T(4,128)(2,1)S(1)}, bf16[1024,4]{0,1:T(4,128)(2,1)}, u32[]{:S(2)}) copy-start(bf16[1024,4]{0,1:T(4,128)(2,1)} %param.24) | copy-start | bytes 24580
  147.2 6.0 %copy-start.7 = (s32[256,2]{0,1:T(2,128)S(1)}, s32[256,2]{0,1:T(2,128)}, u32[]{:S(2)}) copy-start(s32[256,2]{0,1:T(2,128)} %param.20) | copy-start | bytes 6148
  147.2 6.1 %copy-start.9 = (s32[2,256]{1,0:T(2,128)S(1)}, s32[2,256]{1,0:T(2,128)}, u32[]{:S(2)}) copy-start(s32[2,256]{1,0:T(2,128)} %copy-done.8) | copy-start | bytes 6148
  147.2 20.1 %all-to-all-start.1 = ((bf16[4,160,1024]{2,1,0:T(8,128)(2,1)}), bf16[4,160,1024]{2,1,0:T(8,128)(2,1)}, u32[]{:S(2)}, u32[]{:S(2)}) async-start(bf16[4,160,1024]{2,1,0:T(8,128)(2,1)} %fusion.34), calls=%async_computation.1 | async-start | bytes 2621440 | tf_op jit(solution)/shard_map/all_to_all | solution.py:156
Sparse Core Ops, SparseCore 0:
  9.0 49.8 all-gather.2
where the time goes:
time: 184 us; the launch traced here: 183 us
  waiting for transfers between devices  53.7 us (29%)
  local copies, waits for them, and re-layouts  39.4 us (21%)
  matrix products  29.6 us (16%)
  other arithmetic  21.7 us (12%)
  blocking collectives  20.6 us (11%)
  between operations  13.6 us (7%)
  starting transfers between devices  4.44 us (2%)
    all_gather x1, waiting for transfers between devices, on_device(): page_piece = lax.all_gather(page_rows, 'req', axis=0, tiled=True)  39.1 us
    all_to_all x1, blocking collectives, on_device(): lax.all_to_all(buffer, 'expert', split_axis=0, concat_axis=0, tiled=True)  20.6 us
    dynamic_slice x6, local copies, waits for them, and re-layouts, on_device(): result, unused = lax.scan(add_block, initial, (blocks, block_pos))  15.5 us
    dot_general x2, matrix products, add_block(): jnp.einsum('hrk,khd->hrd', weights.astype(jnp.bfloat16), value_rows, pref...  14 us
    all_to_all x1, waiting for transfers between devices, on_device(): lax.all_to_all(expert_done, 'expert', split_axis=0, concat_axis=0, tiled=...  13.9 us
    while x10, local copies, waits for them, and re-layouts  7.6 us
    slice x2, local copies, waits for them, and re-layouts, add_block(): value_rows = block_rows[:, HD:].reshape(step_len, HEADS, HEAD_DIM)  5.29 us
    gather x1, local copies, waits for them, and re-layouts, on_device(): picked_rows = flat_rows[jnp.maximum(slot_ids, 0)]  4.97 us
  transfers between devices with their start and end apart: 2, of which 2 were waited for; matrix products, arithmetic and copies ran while one was open for 8% of the time, Pallas kernels for 0%

commit v1 on v0

--- a/solution.py
+++ b/solution.py
@@ -82,7 +82,26 @@
     )
     start_value = jnp.swapaxes(own_value, 0, 1).astype(jnp.float32)
     initial = (own_score, jnp.ones_like(own_score), start_value)
-    page_piece = lax.all_gather(page_rows, "req", axis=0, tiled=True)
+    r2, shaped, e_next = (lax.axis_size("req"), lax.axis_index("req"), page_rows.shape[0])
+    x_new = o_now = page_rows
+    page_piece = lax.dynamic_update_slice_in_dim(
+        jnp.zeros(
+            [m * r2 if q == 0 else m for q, m in enumerate(page_rows.shape)], page_rows.dtype
+        ),
+        page_rows,
+        shaped * e_next,
+        axis=0,
+    )
+    for jj in range(1, r2 // 2 + 1):
+        x_new = lax.ppermute(x_new, axis_name="req", perm=[(q, (q + 1) % r2) for q in range(r2)])
+        page_piece = lax.dynamic_update_slice_in_dim(
+            page_piece, x_new, (shaped - jj) % r2 * e_next, axis=0
+        )
+        if 2 * jj < r2:
+            o_now = lax.ppermute(o_now, "req", perm=[(q, (q - 1) % r2) for q in range(r2)])
+            page_piece = lax.dynamic_update_slice_in_dim(
+                page_piece, o_now, (shaped + jj) % r2 * e_next, axis=0
+            )
     piece_len = page_piece.shape[0]
     step_len = block_size(piece_len, 512)
     positions = key_positions(table_row, piece_len, PAGE)

time: 184 us -> 169 us (0.918)
  the two profiles are of different devices: /device:TPU:0 before, /device:TPU:8 now
where the time goes in v1:
time: 169 us; the launch traced here: 168 us
  local copies, waits for them, and re-layouts  52.7 us (31%)
  matrix products  29.5 us (17%)
  waiting for transfers between devices  27 us (16%)
  blocking collectives  21.8 us (13%)
  other arithmetic  21.5 us (13%)
  starting transfers between devices  15.3 us (9%)
    all_to_all x1, blocking collectives, on_device(): lax.all_to_all(buffer, 'expert', split_axis=0, concat_axis=0, tiled=True)  21.8 us
    all_to_all x1, waiting for transfers between devices, on_device(): lax.all_to_all(expert_done, 'expert', split_axis=0, concat_axis=0, tiled=...  15.5 us
    dynamic_slice x6, local copies, waits for them, and re-layouts, on_device(): result, unused = lax.scan(add_block, initial, (blocks, block_pos))  15.5 us
    dot_general x2, matrix products, add_block(): jnp.einsum('hrk,khd->hrd', weights.astype(jnp.bfloat16), value_rows, pref...  13.9 us
    ppermute x4, waiting for transfers between devices, on_device(): lax.ppermute(x_new, axis_name='req', perm=[(q, (q + 1) % r2) for q in ran...  10 us
    while x10, local copies, waits for them, and re-layouts  7.57 us
    ppermute x4, starting transfers between devices, on_device(): lax.ppermute(x_new, axis_name='req', perm=[(q, (q + 1) % r2) for q in ran...  7.48 us
    dynamic_update_slice x4, local copies, waits for them, and re-layouts, on_device(): lax.dynamic_update_slice_in_dim(page_piece, x_new, (shaped - jj) % r2 * e...  5.5 us
  transfers between devices with their start and end apart: 8, of which 5 were waited for; matrix products, arithmetic and copies ran while one was open for 16% of the time, Pallas kernels for 0%

profile of v1, /device:TPU:8, one launch (start us, length us, event | category | flops | bytes accessed | tf_op | source)
XLA Modules:
  0.0 168.1 jit_solution(6931001897559784297)
XLA Ops:
  0.1 1.7 %collective-permute-start.1 = (bf16[128,2048]{1,0:T(8,128)(2,1)}, bf16[128,2048]{1,0:T(8,128)(2,1)}, u32[]{:S(2)}, u32[]{:S(2)}) collective-permute-start(bf16[128,2048]{1,0:T(8,128)(2,1)} %bitcast.113), channel_id=1, source_target_pairs={{0,7},{1,0},{2,1},{3,2},{4,3},{5,4},{6,5},{7,6},{8,15},{9,8},{10,9... | collective-permute-start | bytes 1572872 | tf_op jit(solution)/shard_map/ppermute | solution.py:101
  1.8 2.3 %slice_convert_fusion = (f32[256,1024]{1,0:T(8,128)}, bf16[256,1024]{1,0:T(8,128)(2,1)S(1)}) fusion(bf16[256,2048]{1,0:T(8,128)(2,1)} %param.16), kind=kLoop, calls=%fused_computation.55 | loop fusion | flops 262144 | bytes 2621440 | tf_op jit(solution)/shard_map/convert_element_type | solution.py:83
  4.1 1.0 copy.42
  5.1 1.2 copy.40
  7.2 1.2 fusion.42
  9.9 2.6 %collective-permute-done = bf16[128,2048]{1,0:T(8,128)(2,1)} collective-permute-done((bf16[128,2048]{1,0:T(8,128)(2,1)}, bf16[128,2048]{1,0:T(8,128)(2,1)}, u32[]{:S(2)}, u32[]{:S(2)}) %collective-permute-start) | collective-permute-done | bytes 524320 | tf_op jit(solution)/shard_map/ppermute | solution.py:96
  12.4 2.5 %broadcast_in_dim.93 = bf16[1024,2048]{1,0:T(8,128)(2,1)} broadcast(bf16[]{:T(256)} %constant.112.clone.1), dimensions={} | broadcast | bytes 4194306 | tf_op jit(solution)/shard_map/broadcast_in_dim | solution.py:88
  15.7 1.8 %collective-permute-start.3 = (bf16[128,2048]{1,0:T(8,128)(2,1)}, bf16[128,2048]{1,0:T(8,128)(2,1)}, u32[]{:S(2)}, u32[]{:S(2)}) collective-permute-start(bf16[128,2048]{1,0:T(8,128)(2,1)} %collective-permute-done.1), channel_id=1, source_target_pairs={{0,7},{1,0},{2,1},{3,2},{4,3},{5,4},{6,5},{7,6},{8,15},{9,8},{10,9... | collective-permute-start | bytes 1572872 | tf_op jit(solution)/shard_map/ppermute | solution.py:101
  17.5 1.0 fusion.43
  18.5 2.6 %copy.29 = f32[256,1024]{0,1:T(8,128)} copy(f32[256,1024]{1,0:T(8,128)} %get-tuple-element.119) | data formatting | bytes 2097152 | tf_op jit(solution)/shard_map/convert_element_type | solution.py:83
  21.7 4.7 %collective-permute-start.4 = (bf16[128,2048]{1,0:T(8,128)(2,1)}, bf16[128,2048]{1,0:T(8,128)(2,1)S(1)}, u32[]{:S(2)}, u32[]{:S(2)}) collective-permute-start(bf16[128,2048]{1,0:T(8,128)(2,1)} %collective-permute-done.2), channel_id=1, source_target_pairs={{0,1},{1,2},{2,3},{3,4},{4,5},{5,6},{6,7},{7,0},{8,9},{9,10},{10,1... | collective-permute-start | bytes 1572872 | tf_op jit(solution)/shard_map/ppermute | solution.py:96
  26.4 1.9 %constant_dynamic-update-slice_fusion.6 = bf16[1024,2048]{1,0:T(8,128)(2,1)} fusion(bf16[1024,2048]{1,0:T(8,128)(2,1)} %constant_dynamic-update-slice_fusion.7, bf16[128,2048]{1,0:T(8,128)(2,1)} %collective-permute-done, s32[]{:T(128)S(6)} %select_n.102), kind=kLoop, calls=%fused_computation.92 | loop fusion | bytes 1048580 | tf_op jit(solution)/shard_map/dynamic_update_slice | solution.py:97
  28.3 1.9 %constant_dynamic-update-slice_fusion.5 = bf16[1024,2048]{1,0:T(8,128)(2,1)} fusion(bf16[1024,2048]{1,0:T(8,128)(2,1)} %constant_dynamic-update-slice_fusion.6, bf16[128,2048]{1,0:T(8,128)(2,1)} %collective-permute-done.1, s32[]{:T(128)S(6)} %select_n.104), kind=kLoop, calls=%fused_computation.91 | loop fusion | bytes 1048580 | tf_op jit(solution)/shard_map/dynamic_update_slice | solution.py:102
  30.2 1.9 %constant_dynamic-update-slice_fusion.4 = bf16[1024,2048]{1,0:T(8,128)(2,1)} fusion(bf16[1024,2048]{1,0:T(8,128)(2,1)} %constant_dynamic-update-slice_fusion.5, bf16[128,2048]{1,0:T(8,128)(2,1)} %collective-permute-done.2, s32[]{:T(128)S(6)} %select_n.106), kind=kLoop, calls=%fused_computation.90 | loop fusion | bytes 1048580 | tf_op jit(solution)/shard_map/dynamic_update_slice | solution.py:97
  32.1 1.4 collective-permute-done.4
  33.6 2.7 %collective-permute-start.6 = (bf16[128,2048]{1,0:T(8,128)(2,1)S(1)}, bf16[128,2048]{1,0:T(8,128)(2,1)S(1)}, u32[]{:S(2)}, u32[]{:S(2)}) collective-permute-start(bf16[128,2048]{1,0:T(8,128)(2,1)S(1)} %collective-permute-done.4), channel_id=1, source_target_pairs={{0,1},{1,2},{2,3},{3,4},{4,5},{5,6},{6,7},{7,0},{8,9},{9,10},{10,1... | collective-permute-start | bytes 1572872 | tf_op jit(solution)/shard_map/ppermute | solution.py:96
  36.3 1.9 %constant_dynamic-update-slice_fusion.3 = bf16[1024,2048]{1,0:T(8,128)(2,1)} fusion(bf16[1024,2048]{1,0:T(8,128)(2,1)} %constant_dynamic-update-slice_fusion.4, bf16[128,2048]{1,0:T(8,128)(2,1)} %collective-permute-done.3, s32[]{:T(128)S(6)} %select_n.108), kind=kLoop, calls=%fused_computation.89 | loop fusion | bytes 1048580 | tf_op jit(solution)/shard_map/dynamic_update_slice | solution.py:102
  39.0 1.5 collective-permute-done.5
  41.3 6.0 %collective-permute-done.6 = bf16[128,2048]{1,0:T(8,128)(2,1)S(1)} collective-permute-done((bf16[128,2048]{1,0:T(8,128)(2,1)S(1)}, bf16[128,2048]{1,0:T(8,128)(2,1)S(1)}, u32[]{:S(2)}, u32[]{:S(2)}) %collective-permute-start.6) | collective-permute-done | bytes 524320 | tf_op jit(solution)/shard_map/ppermute | solution.py:96
  48.1 54.2 %while.15 = (s32[]{:T(128)}, f32[16,256]{1,0:T(8,128)}, f32[16,256]{1,0:T(8,128)}, f32[16,256,64]{1,2,0:T(8,128)}, s32[2,512]{1,0:T(2,128)}, /*index=5*/s32[256]...) while((s32[]{:T(128)}, f32[16,256]{1,0:T(8,128)}, ...), condition=%wide.region_5.6_spmd.clone, body=%wide.region_2.5_spmd.clone.sunk | while | flops 560607232 | bytes 76881064 | solution.py:134
  49.6 3.2 %constant_dynamic-slice_fusion.5 = bf16[1,512,2048]{2,1,0:T(8,128)(2,1)} fusion(bf16[2,512,2048]{2,1,0:T(8,128)(2,1)} %get-tuple-element.210, s32[]{:T(128)} %get-tuple-element.194), kind=kLoop, calls=%fused_computation.13.clone.1 | loop fusion | bytes 4194308 | tf_op jit(solution)/shard_map/while/body/jit(dynamic_index_in_dim)/dynamic_slice | solution.py:134
  52.8 3.9 %copy.46 = bf16[1,512,2048]{1,2,0:T(8,128)(2,1)} copy(bf16[1,512,2048]{2,1,0:T(8,128)(2,1)} %constant_dynamic-slice_fusion.5) | data formatting | bytes 4194304 | tf_op jit(solution)/shard_map/while/body/jit(dynamic_index_in_dim)/dynamic_slice | solution.py:134
  56.7 2.6 %fusion.80 = (bf16[512,1024]{0,1:T(8,128)(2,1)}, bf16[512,1024]{0,1:T(8,128)(2,1)S(1)}) fusion(bf16[512,2048]{0,1:T(8,128)(2,1)} %bitcast.104), kind=kLoop, calls=%fused_computation.102.clone.1 | loop fusion | bytes 4194304 | tf_op jit(solution)/shard_map/while/body/eval_jaxpr/slice | solution.py:115
  59.3 1.5 fusion.81
  60.9 3.2 %copy-done.1 = f32[16,512,256]{2,1,0:T(8,128)} copy-done((f32[16,512,256]{2,1,0:T(8,128)}, f32[16,512,256]{2,1,0:T(8,128)S(1)}, u32[]{:S(2)}) %copy-start.1) | copy-done | bytes 8388632 | tf_op jit(solution)/shard_map/while
  64.0 2.3 %fusion.82 = f32[16,256]{1,0:T(8,128)} fusion(f32[16,512,256]{2,1,0:T(8,128)S(1)} %get-tuple-element.180, f32[16,256]{1,0:T(8,128)S(1)} %max.10, pred[256,512]{0,1:T(8,128)(4,1)S(1)} %broadcast_compare_fusion.3), kind=kLoop, calls=%fused_computation.4.clone.1 | loop fusion | flops 8384512 | bytes 8552448 | tf_op jit(solution)/shard_map/while/body/eval_jaxpr/reduce_sum | solution.py:125
  66.3 1.3 fusion.83
  67.7 7.0 %fusion.84 = f32[16,256,64]{1,2,0:T(8,128)} fusion(bf16[512,16,64]{0,2,1:T(8,128)(2,1)} %bitcast.106, f32[16,512,256]{2,1,0:T(8,128)} %copy-done.1, f32[16,256]{1,0:T(8,128)S(1)} %max.10, pred[256,512]{0,1:T(8,128)(4,1)S(1)} %broadcast_compare_fusion.3, f32[16,256,64]{1,2,0:T(8,128)} %get-tuple-element.197, f32[16,256]{1,0:T(8,128)S(1)} %get-tuple-element.183), kind=kOutput, calls=%fused_computation.8.clone.1 | convolution fusion | flops 277348352 | bytes 11698176 | tf_op jit(solution)/shard_map/while/body/eval_jaxpr/hrk,khd->hrd/dot_general | solution.py:126
  76.7 3.2 %constant_dynamic-slice_fusion.5 = bf16[1,512,2048]{2,1,0:T(8,128)(2,1)} fusion(bf16[2,512,2048]{2,1,0:T(8,128)(2,1)} %get-tuple-element.210, s32[]{:T(128)} %get-tuple-element.194), kind=kLoop, calls=%fused_computation.13.clone.1 | loop fusion | bytes 4194308 | tf_op jit(solution)/shard_map/while/body/jit(dynamic_index_in_dim)/dynamic_slice | solution.py:134
  79.9 3.9 %copy.46 = bf16[1,512,2048]{1,2,0:T(8,128)(2,1)} copy(bf16[1,512,2048]{2,1,0:T(8,128)(2,1)} %constant_dynamic-slice_fusion.5) | data formatting | bytes 4194304 | tf_op jit(solution)/shard_map/while/body/jit(dynamic_index_in_dim)/dynamic_slice | solution.py:134
  83.8 2.6 %fusion.80 = (bf16[512,1024]{0,1:T(8,128)(2,1)}, bf16[512,1024]{0,1:T(8,128)(2,1)S(1)}) fusion(bf16[512,2048]{0,1:T(8,128)(2,1)} %bitcast.104), kind=kLoop, calls=%fused_computation.102.clone.1 | loop fusion | bytes 4194304 | tf_op jit(solution)/shard_map/while/body/eval_jaxpr/slice | solution.py:115
  86.5 1.5 fusion.81
  88.0 3.2 %copy-done.1 = f32[16,512,256]{2,1,0:T(8,128)} copy-done((f32[16,512,256]{2,1,0:T(8,128)}, f32[16,512,256]{2,1,0:T(8,128)S(1)}, u32[]{:S(2)}) %copy-start.1) | copy-done | bytes 8388632 | tf_op jit(solution)/shard_map/while
  91.2 2.3 %fusion.82 = f32[16,256]{1,0:T(8,128)} fusion(f32[16,512,256]{2,1,0:T(8,128)S(1)} %get-tuple-element.180, f32[16,256]{1,0:T(8,128)S(1)} %max.10, pred[256,512]{0,1:T(8,128)(4,1)S(1)} %broadcast_compare_fusion.3), kind=kLoop, calls=%fused_computation.4.clone.1 | loop fusion | flops 8384512 | bytes 8552448 | tf_op jit(solution)/shard_map/while/body/eval_jaxpr/reduce_sum | solution.py:125
  93.4 1.4 fusion.83
  94.8 7.0 %fusion.84 = f32[16,256,64]{1,2,0:T(8,128)} fusion(bf16[512,16,64]{0,2,1:T(8,128)(2,1)} %bitcast.106, f32[16,512,256]{2,1,0:T(8,128)} %copy-done.1, f32[16,256]{1,0:T(8,128)S(1)} %max.10, pred[256,512]{0,1:T(8,128)(4,1)S(1)} %broadcast_compare_fusion.3, f32[16,256,64]{1,2,0:T(8,128)} %get-tuple-element.197, f32[16,256]{1,0:T(8,128)S(1)} %get-tuple-element.183), kind=kOutput, calls=%fused_computation.8.clone.1 | convolution fusion | flops 277348352 | bytes 11698176 | tf_op jit(solution)/shard_map/while/body/eval_jaxpr/hrk,khd->hrd/dot_general | solution.py:126
  102.4 1.5 divide_convert_fusion
  103.9 2.7 %multiply_reduce_fusion.1 = (f32[256]{0:T(256)S(1)}, f32[256,1024]{1,0:T(8,128)S(1)}) fusion(bf16[256,1024]{0,1:T(8,128)(2,1)S(1)} %bitcast.111, bf16[1024,1024]{1,0:T(8,128)(2,1)} %param.22, bf16[256,1024]{1,0:T(8,128)(2,1)} %param.21), kind=kOutput, calls=%fused_computation.51 | convolution fusion | flops 537919232 | bytes 4195328 | tf_op jit(solution)/shard_map/dot_general | solution.py:142
  106.6 1.0 copy-done.2
  108.2 21.8 %all_to_all.10 = bf16[4,160,1024]{2,1,0:T(8,128)(2,1)S(1)} all-to-all(bf16[4,160,1024]{2,1,0:T(8,128)(2,1)S(1)} %bitcast.108), channel_id=1, replica_groups=mesh['expert'=4,'req'=8] {'expert'}, dimensions={0} | all-to-all | bytes 2621440 | tf_op jit(solution)/shard_map/all_to_all | solution.py:162
  130.0 3.9 %fusion.14 = f32[4,1,160,2816]{3,2,0,1:T(8,128)S(1)} fusion(bf16[4,160,1024]{2,1,0:T(8,128)(2,1)S(1)} %all_to_all.10, bf16[1,1024,2816]{2,1,0:T(8,128)(2,1)S(1)} %bitcast.119), kind=kOutput, calls=%fused_computation.20 | convolution fusion | flops 3690987520 | bytes 14286848 | tf_op jit(solution)/shard_map/slnd,ldf->slnf/dot_general | solution.py:167
  133.9 3.6 %fusion.34 = bf16[4,160,1024]{2,1,0:T(8,128)(2,1)} fusion(bf16[1,1408,1024]{2,1,0:T(8,128)(2,1)S(1)} %copy-done, f32[4,1,160,2816]{3,2,0,1:T(8,128)S(1)} %fusion.14), kind=kOutput, calls=%fused_computation.39 | convolution fusion | flops 1855160320 | bytes 11403264 | tf_op jit(solution)/shard_map/slnf,lfd->slnd/dot_general | solution.py:171
  137.6 4.3 %all-to-all-start.1 = ((bf16[4,160,1024]{2,1,0:T(8,128)(2,1)}), bf16[4,160,1024]{2,1,0:T(8,128)(2,1)}, u32[]{:S(2)}, u32[]{:S(2)}) async-start(bf16[4,160,1024]{2,1,0:T(8,128)(2,1)} %fusion.34), calls=%async_computation.1 | async-start | bytes 2621440 | tf_op jit(solution)/shard_map/all_to_all | solution.py:175
  141.9 1.5 fusion.56
  143.6 15.5 %all-to-all-done.1 = bf16[4,160,1024]{2,1,0:T(8,128)(2,1)} async-done(((bf16[4,160,1024]{2,1,0:T(8,128)(2,1)}), bf16[4,160,1024]{2,1,0:T(8,128)(2,1)}, u32[]{:S(2)}, u32[]{:S(2)}) %all-to-all-start.1) | async-done | bytes 1310752 | tf_op jit(solution)/shard_map/all_to_all | solution.py:175
  159.1 5.0 %gather_fusion = bf16[512,1024]{1,0:T(8,128)(2,1)} fusion(bf16[640,1024]{1,0:T(8,128)(2,1)} %bitcast.26, s32[1024]{0:T(1024)S(1)} %pad_clamp_fusion), kind=kCustom, calls=%fused_computation | custom fusion | bytes 2099200 | tf_op jit(solution)/shard_map/gather | solution.py:177
  164.1 1.6 fusion.28
  165.7 1.4 multiply_reduce_fusion
  (79 shorter events, 12.2 us)
Async XLA Ops:
  0.0 133.9 %copy-start = (bf16[1,1408,1024]{2,1,0:T(8,128)(2,1)S(1)}, bf16[1,1408,1024]{2,1,0:T(8,128)(2,1)}, u32[]{:S(2)}) copy-start(bf16[1,1408,1024]{2,1,0:T(8,128)(2,1)} %param.26) | copy-start | bytes 8650756
  0.0 6.4 %copy-start.15 = (s32[1,8]{1,0:T(1,128)S(1)}, s32[1,8]{1,0:T(1,128)}, u32[]{:S(2)}) copy-start(s32[1,8]{1,0:T(1,128)} %param.18) | copy-start | bytes 100
  0.0 7.2 %copy-start.7 = (s32[256,2]{0,1:T(2,128)S(1)}, s32[256,2]{0,1:T(2,128)}, u32[]{:S(2)}) copy-start(s32[256,2]{0,1:T(2,128)} %param.20) | copy-start | bytes 6148
  0.0 12.4 %collective-permute-start = (bf16[128,2048]{1,0:T(8,128)(2,1)}, bf16[128,2048]{1,0:T(8,128)(2,1)}, u32[]{:S(2)}, u32[]{:S(2)}) collective-permute-start(bf16[128,2048]{1,0:T(8,128)(2,1)} %bitcast.112), channel_id=1, source_target_pairs={{0,1},{1,2},{2,3},{3,4},{4,5},{5,6},{6,7},{7,0},{8,9},{9,10},{10,1... | collective-permute-start | bytes 1572872 | tf_op jit(solution)/shard_map/ppermute | solution.py:96
  0.1 15.6 %collective-permute-start.1 = (bf16[128,2048]{1,0:T(8,128)(2,1)}, bf16[128,2048]{1,0:T(8,128)(2,1)}, u32[]{:S(2)}, u32[]{:S(2)}) collective-permute-start(bf16[128,2048]{1,0:T(8,128)(2,1)} %bitcast.113), channel_id=1, source_target_pairs={{0,7},{1,0},{2,1},{3,2},{4,3},{5,4},{6,5},{7,6},{8,15},{9,8},{10,9... | collective-permute-start | bytes 1572872 | tf_op jit(solution)/shard_map/ppermute | solution.py:101
  8.4 12.7 %copy-start.13 = (bf16[1024]{0:T(1024)(128)(2,1)S(1)}, bf16[1024]{0:T(1024)(128)(2,1)}, u32[]{:S(2)}) copy-start(bf16[1024]{0:T(1024)(128)(2,1)} %param.23) | copy-start | bytes 6148
  8.7 19.6 %copy-start.9 = (s32[2,256]{1,0:T(2,128)}, s32[2,256]{1,0:T(2,128)S(1)}, u32[]{:S(2)}) copy-start(s32[2,256]{1,0:T(2,128)S(1)} %reshape.127) | copy-start | bytes 6148
  9.9 5.0 %copy-start.5 = (bf16[1,128,2048]{2,1,0:T(8,128)(2,1)S(1)}, bf16[1,128,2048]{2,1,0:T(8,128)(2,1)}, u32[]{:S(2)}) copy-start(bf16[1,128,2048]{2,1,0:T(8,128)(2,1)} %param.17) | copy-start | bytes 1572868
  12.4 9.3 %collective-permute-start.2 = (bf16[128,2048]{1,0:T(8,128)(2,1)}, bf16[128,2048]{1,0:T(8,128)(2,1)}, u32[]{:S(2)}, u32[]{:S(2)}) collective-permute-start(bf16[128,2048]{1,0:T(8,128)(2,1)} %collective-permute-done), channel_id=1, source_target_pairs={{0,1},{1,2},{2,3},{3,4},{4,5},{5,6},{6,7},{7,0},{8,9},{9,10},{10,1... | collective-permute-start | bytes 1572872 | tf_op jit(solution)/shard_map/ppermute | solution.py:96
  15.7 14.5 %collective-permute-start.3 = (bf16[128,2048]{1,0:T(8,128)(2,1)}, bf16[128,2048]{1,0:T(8,128)(2,1)}, u32[]{:S(2)}, u32[]{:S(2)}) collective-permute-start(bf16[128,2048]{1,0:T(8,128)(2,1)} %collective-permute-done.1), channel_id=1, source_target_pairs={{0,7},{1,0},{2,1},{3,2},{4,3},{5,4},{6,5},{7,6},{8,15},{9,8},{10,9... | collective-permute-start | bytes 1572872 | tf_op jit(solution)/shard_map/ppermute | solution.py:101
  21.7 11.9 %collective-permute-start.4 = (bf16[128,2048]{1,0:T(8,128)(2,1)}, bf16[128,2048]{1,0:T(8,128)(2,1)S(1)}, u32[]{:S(2)}, u32[]{:S(2)}) collective-permute-start(bf16[128,2048]{1,0:T(8,128)(2,1)} %collective-permute-done.2), channel_id=1, source_target_pairs={{0,1},{1,2},{2,3},{3,4},{4,5},{5,6},{6,7},{7,0},{8,9},{9,10},{10,1... | collective-permute-start | bytes 1572872 | tf_op jit(solution)/shard_map/ppermute | solution.py:96
  30.2 10.3 %collective-permute-start.5 = (bf16[128,2048]{1,0:T(8,128)(2,1)}, bf16[128,2048]{1,0:T(8,128)(2,1)S(1)}, u32[]{:S(2)}, u32[]{:S(2)}) collective-permute-start(bf16[128,2048]{1,0:T(8,128)(2,1)} %collective-permute-done.3), channel_id=1, source_target_pairs={{0,7},{1,0},{2,1},{3,2},{4,3},{5,4},{6,5},{7,6},{8,15},{9,8},{10,9... | collective-permute-start | bytes 1572872 | tf_op jit(solution)/shard_map/ppermute | solution.py:101
  33.6 13.7 %collective-permute-start.6 = (bf16[128,2048]{1,0:T(8,128)(2,1)S(1)}, bf16[128,2048]{1,0:T(8,128)(2,1)S(1)}, u32[]{:S(2)}, u32[]{:S(2)}) collective-permute-start(bf16[128,2048]{1,0:T(8,128)(2,1)S(1)} %collective-permute-done.4), channel_id=1, source_target_pairs={{0,1},{1,2},{2,3},{3,4},{4,5},{5,6},{6,7},{7,0},{8,9},{9,10},{10,1... | collective-permute-start | bytes 1572872 | tf_op jit(solution)/shard_map/ppermute | solution.py:96
  59.3 1.5 copy-start.3
  60.8 3.2 %copy-start.1 = (f32[16,512,256]{2,1,0:T(8,128)}, f32[16,512,256]{2,1,0:T(8,128)S(1)}, u32[]{:S(2)}) copy-start(f32[16,512,256]{2,1,0:T(8,128)S(1)} %get-tuple-element.180) | copy-start | bytes 25165828 | tf_op jit(solution)/shard_map/while
  86.5 1.5 copy-start.3
  87.9 3.2 %copy-start.1 = (f32[16,512,256]{2,1,0:T(8,128)}, f32[16,512,256]{2,1,0:T(8,128)S(1)}, u32[]{:S(2)}) copy-start(f32[16,512,256]{2,1,0:T(8,128)S(1)} %get-tuple-element.180) | copy-start | bytes 25165828 | tf_op jit(solution)/shard_map/while
  102.4 5.2 %copy-start.4 = (bf16[640,256]{1,0:T(8,128)(2,1)S(1)}, bf16[640,256]{1,0:T(8,128)(2,1)}, u32[]{:S(2)}) copy-start(bf16[640,256]{1,0:T(8,128)(2,1)} %fusion.43) | copy-start | bytes 983044
  102.4 5.2 %copy-start.6 = (f32[1024]{0:T(1024)S(1)}, f32[1024]{0:T(1024)}, u32[]{:S(2)}) copy-start(f32[1024]{0:T(1024)} %convert_element_type.81) | copy-start | bytes 12292
  102.4 27.6 %slice-start = ((s8[5767168]{0:T(1024)(128)(4,1)}), s8[4194304]{0:T(1024)(128)(4,1)S(1)}, s32[]{:S(2)}) async-start(s8[5767168]{0:T(1024)(128)(4,1)} %bitcast.118), calls=%async_computation.2 | async-start | bytes 8388608
  103.9 26.1 %slice-start.1 = ((s8[5767168]{0:T(1024)(128)(4,1)}), s8[1572864]{0:T(1024)(128)(4,1)S(1)}, s32[]{:S(2)}) async-start(s8[5767168]{0:T(1024)(128)(4,1)} %bitcast.118), calls=%async_computation.3 | async-start | bytes 3145728
  106.6 1.0 copy-start.2
  133.9 8.0 %copy-start.12 = (s32[1,2,2,128]{3,2,1,0:T(2,128)S(1)}, s32[1,2,2,128]{3,2,1,0:T(2,128)}, u32[]{:S(2)}) copy-start(s32[1,2,2,128]{3,2,1,0:T(2,128)} %get-tuple-element.113) | copy-start | bytes 6148
  133.9 8.0 %copy-start.14 = (bf16[1024]{0:T(1024)(128)(2,1)S(1)}, bf16[1024]{0:T(1024)(128)(2,1)}, u32[]{:S(2)}) copy-start(bf16[1024]{0:T(1024)(128)(2,1)} %param.27) | copy-start | bytes 6148
  133.9 8.0 %copy-start.11 = (bf16[1024,4]{0,1:T(4,128)(2,1)S(1)}, bf16[1024,4]{0,1:T(4,128)(2,1)}, u32[]{:S(2)}) copy-start(bf16[1024,4]{0,1:T(4,128)(2,1)} %param.24) | copy-start | bytes 24580
  133.9 9.5 %copy-start.8 = (s32[256,2]{0,1:T(2,128)S(1)}, s32[256,2]{0,1:T(2,128)}, u32[]{:S(2)}) copy-start(s32[256,2]{0,1:T(2,128)} %param.20) | copy-start | bytes 6148
  133.9 9.7 %copy-start.10 = (s32[2,256]{1,0:T(2,128)S(1)}, s32[2,256]{1,0:T(2,128)}, u32[]{:S(2)}) copy-start(s32[2,256]{1,0:T(2,128)} %copy-done.9) | copy-start | bytes 6148
  137.6 21.5 %all-to-all-start.1 = ((bf16[4,160,1024]{2,1,0:T(8,128)(2,1)}), bf16[4,160,1024]{2,1,0:T(8,128)(2,1)}, u32[]{:S(2)}, u32[]{:S(2)}) async-start(bf16[4,160,1024]{2,1,0:T(8,128)(2,1)} %fusion.34), calls=%async_computation.1 | async-start | bytes 2621440 | tf_op jit(solution)/shard_map/all_to_all | solution.py:175
